TPU v7x, 32 devices: a whole 2x2x4 slice. The times are simulated.
32 devices in a mesh: seq: 4 (over z), dp: 8 (over y, x, core).
Axes of the slice: x: 2, y: 2, z: 4, core: 2. Of those that a mesh axis runs over, the one named last changes fastest.
Arguments:
- tokens: bfloat16 [8, 1024, 768], P('dp', 'seq'), may hold values from -6 to 6
- qkv_weight: bfloat16 [768, 2304], P('dp'), may hold values from -0.21875 to 0.21875
- proj_weight: bfloat16 [768, 768], P('dp'), may hold values from -0.875 to 0.875
- hidden_weight: bfloat16 [768, 3072], P('dp'), may hold values from -0.21875 to 0.21875
- output_weight: bfloat16 [3072, 768], P('dp'), may hold values from -0.109375 to 0.109375
- first_gain: bfloat16 [768], P('dp'), may hold values from 0.25 to 1.75
- first_bias: bfloat16 [768], P('dp'), may hold values from -2.5 to 2.5
- second_gain: bfloat16 [768], P('dp'), may hold values from 0.25 to 1.75
- second_bias: bfloat16 [768], P('dp'), may hold values from -2.5 to 2.5
- cotangent: bfloat16 [8, 1024, 768], P('dp', 'seq'), may hold values from -6 to 6
Outputs:
- block_out: bfloat16 [8, 1024, 768], P('dp', 'seq')
- tokens_gradient: bfloat16 [8, 1024, 768], P('dp', 'seq')
- qkv_gradient: float32 [768, 2304], P('dp')
- proj_gradient: float32 [768, 768], P('dp')
- hidden_gradient: float32 [768, 3072], P('dp')
- output_gradient: float32 [3072, 768], P('dp')
- first_gain_gradient: float32 [768], P('dp')
- first_bias_gradient: float32 [768], P('dp')
- second_gain_gradient: float32 [768], P('dp')
- second_bias_gradient: float32 [768], P('dp')
All inputs are finite; a program needn't handle non-finite values.
Results may differ from a plain program's by a relative error of at most 0.012.
Values may be sent and summed in bfloat16 or wider, within the bound.
A program may use at most 256 MiB of HBM per device.

v0:
```python
import jax
import jax.numpy as jnp
from jax import lax
from jax.experimental import pallas as pl
from jax.experimental.pallas import tpu as pltpu
from jax.sharding import PartitionSpec as P

HEAD_DIM = 64
LOW = jnp.bfloat16
F32 = jnp.float32


def layer_norm(values, gain, bias):
    average = jnp.mean(values, -1, keepdims=True)
    centred = values - average
    variance = jnp.mean(centred * centred, -1, keepdims=True)
    return centred * lax.rsqrt(variance + 1e-05) * gain + bias


def gelu_tanh(values):
    return jax.nn.gelu(values, approximate=True)


def matmul(left, right):
    return jnp.dot(left, right, preferred_element_type=F32)


def matmul_left_t(left, right):
    return lax.dot_general(left, right, (((0,), (0,)), ((), ())), preferred_element_type=F32)


def matmul_right_t(left, right):
    return lax.dot_general(left, right, (((1,), (1,)), ((), ())), preferred_element_type=F32)


def gather_seq(value):
    return lax.all_gather(value, "seq", axis=0, tiled=True)


def scatter_seq(value):
    return lax.psum_scatter(value.astype(LOW), "seq", scatter_dimension=0, tiled=True).astype(F32)


def remote(src, dst, send, recv, axis, target):
    return pltpu.make_async_remote_copy(
        src_ref=src,
        dst_ref=dst,
        send_sem=send,
        recv_sem=recv,
        device_id={axis: target},
        device_id_type=pl.DeviceIdType.MESH,
    )


def greet(axes):
    barrier = pltpu.get_barrier_semaphore()
    count = 0
    for axis, size in axes:
        me = lax.axis_index(axis)
        for step in range(1, size):
            pl.semaphore_signal(
                barrier,
                inc=1,
                device_id={axis: lax.rem(me + step, size)},
                device_id_type=pl.DeviceIdType.MESH,
            )
            count += 1
    pl.semaphore_wait(barrier, count)


ANY = pl.BlockSpec(memory_space=pl.ANY)
VMEM = pl.BlockSpec(memory_space=pltpu.VMEM)


def params(collective_id):
    return pltpu.CompilerParams(
        collective_id=collective_id, has_side_effects=True, vmem_limit_bytes=32 * 1024 * 1024
    )


def line_gather(parts, source, out, send, recv, own):
    seq = lax.axis_index("seq")
    local = pltpu.make_async_copy(source, out.at[seq], own)
    local.start()

    def hop(way, sign, step):
        origin = lax.rem(seq - sign * step + parts, parts)
        return remote(
            source if step == 0 else out.at[origin],
            out.at[origin],
            send.at[way, step],
            recv.at[way, step],
            "seq",
            lax.rem(seq + sign + parts, parts),
        )

    def sends(sign, step):
        origin = seq - sign * step
        return (seq + sign >= 0) & (seq + sign < parts) & (origin >= 0) & (origin < parts)

    def arrives(sign, step):
        origin = seq - sign * step
        return (origin >= 0) & (origin < parts)

    ways = ((0, 1), (1, -1))
    for way, sign in ways:

        @pl.when(sends(sign, 0))
        def _():
            hop(way, sign, 0).start()

    yield
    for step in range(1, parts):
        for way, sign in ways:

            @pl.when(arrives(sign, step))
            def _():
                origin = lax.rem(seq - sign * step + parts, parts)
                remote(
                    source,
                    out.at[origin],
                    send.at[way, step - 1],
                    recv.at[way, step - 1],
                    "seq",
                    lax.rem(seq + sign + parts, parts),
                ).wait_recv()

            if step < parts - 1:

                @pl.when(sends(sign, step))
                def _():
                    hop(way, sign, step).start()

    yield
    for step in range(parts - 1):
        for way, sign in ways:

            @pl.when(sends(sign, step))
            def _():
                hop(way, sign, step).wait_send()

    local.wait()


def line_reduce(parts, terms, out, stage, land, send, recv):
    seq = lax.axis_index("seq")
    signs = (1, -1)

    def copy(way, dest):
        return remote(
            stage.at[way, dest],
            land.at[way, dest],
            send.at[way, dest],
            recv.at[way, dest],
            "seq",
            lax.rem(seq + signs[way] + parts, parts),
        )

    def passes(way, dest):
        return seq < dest if way == 0 else seq > dest

    def first(way):
        return seq == 0 if way == 0 else seq == parts - 1

    def forward(way, at):
        dest = parts - 1 - at if way == 0 else at

        @pl.when(passes(way, dest) & first(way))
        def _():
            stage[way, dest] = terms[dest]
            copy(way, dest).start()

        @pl.when(passes(way, dest) & ~first(way))
        def _():
            copy(way, dest).wait_recv()
            stage[way, dest] = (
                terms[dest].astype(F32) + land[way, dest].astype(F32)
            ).astype(stage.dtype)
            copy(way, dest).start()

    def order(lead):
        forward(lead, 0)
        for at in range(parts - 1):
            forward(1 - lead, at)
            if at + 1 < parts - 1:
                forward(lead, at + 1)

    @pl.when(2 * seq < parts)
    def _():
        order(0)

    @pl.when(2 * seq >= parts)
    def _():
        order(1)

    yield
    out[...] = terms[seq].astype(F32)
    for way in range(2):

        @pl.when(~first(way))
        def _():
            copy(way, seq).wait_recv()
            out[...] += land[way, seq].astype(F32)

    for way in range(2):
        for dest in range(parts):

            @pl.when(passes(way, dest))
            def _():
                copy(way, dest).wait_send()


def run(*generators):
    live = list(generators)
    while live:
        live = [item for item in live if next(item, "end") != "end"]


def start_gather(parts, groups, tokens, pieces):
    count = len(pieces)
    half = groups // 2

    def kernel(*refs):
        token_in, piece_in = refs[0], refs[1 : 1 + count]
        token_out, piece_out = refs[1 + count], refs[2 + count : 2 + 2 * count]
        token_send, token_recv, send, recv, pair_send, pair_recv, own = refs[2 + 2 * count :]
        dp = lax.axis_index("dp")
        sibling = dp + 1 - 2 * lax.rem(dp, 2)
        greet((("seq", parts), ("dp", groups)))
        far, near, local = [], [], []
        for k in range(count):
            for step in range(1, half):
                copy = remote(
                    piece_in[k],
                    piece_out[k].at[dp],
                    send.at[k, step],
                    recv.at[k, step],
                    "dp",
                    lax.rem(dp + 2 * step, groups),
                )
                copy.start()
                far.append((k, step, copy))
        line = line_gather(parts, token_in, token_out, token_send, token_recv, own.at[count])
        next(line)
        for k in range(count):
            copy = remote(
                piece_in[k],
                piece_out[k].at[dp],
                pair_send.at[k, 0],
                pair_recv.at[k, 0],
                "dp",
                sibling,
            )
            copy.start()
            near.append(copy)
            copy = pltpu.make_async_copy(piece_in[k], piece_out[k].at[dp], own.at[k])
            copy.start()
            local.append(copy)
        for k, step, copy in far:
            copy.wait_recv()
            origin = lax.rem(dp - 2 * step + groups, groups)
            passed = remote(
                piece_out[k].at[origin],
                piece_out[k].at[origin],
                pair_send.at[k, step],
                pair_recv.at[k, step],
                "dp",
                sibling,
            )
            passed.start()
            near.append(passed)
        for _, _, copy in far:
            copy.wait_send()
        for copy in near + local:
            copy.wait()
        run(line)

    return pl.pallas_call(
        kernel,
        out_shape=[jax.ShapeDtypeStruct((parts,) + tokens.shape, tokens.dtype)]
        + [jax.ShapeDtypeStruct((groups,) + item.shape, item.dtype) for item in pieces],
        in_specs=[ANY] * (1 + count),
        out_specs=[ANY] * (1 + count),
        scratch_shapes=[
            pltpu.SemaphoreType.DMA((2, parts)),
            pltpu.SemaphoreType.DMA((2, parts)),
            pltpu.SemaphoreType.DMA((count, half)),
            pltpu.SemaphoreType.DMA((count, half)),
            pltpu.SemaphoreType.DMA((count, half)),
            pltpu.SemaphoreType.DMA((count, half)),
            pltpu.SemaphoreType.DMA((count + 1,)),
        ],
        compiler_params=params(0),
        name="start_gather",
    )(tokens, *pieces)


def seq_gather(parts, value, collective_id, name):
    def kernel(in_ref, out_ref, send, recv, own):
        greet((("seq", parts),))
        run(line_gather(parts, in_ref, out_ref, send, recv, own))

    return pl.pallas_call(
        kernel,
        out_shape=jax.ShapeDtypeStruct((parts,) + value.shape, value.dtype),
        in_specs=[ANY],
        out_specs=ANY,
        scratch_shapes=[
            pltpu.SemaphoreType.DMA((2, parts)),
            pltpu.SemaphoreType.DMA((2, parts)),
            pltpu.SemaphoreType.DMA,
        ],
        compiler_params=params(collective_id),
        name=name,
    )(value)


def line_scratch(parts, terms):
    return [
        pltpu.VMEM((2,) + terms.shape, terms.dtype),
        pltpu.VMEM((2,) + terms.shape, terms.dtype),
        pltpu.SemaphoreType.DMA((2, parts)),
        pltpu.SemaphoreType.DMA((2, parts)),
    ]


def seq_reduce(parts, terms, collective_id, name):
    def kernel(in_ref, out_ref, stage, land, send, recv):
        greet((("seq", parts),))
        run(line_reduce(parts, in_ref, out_ref, stage, land, send, recv))

    return pl.pallas_call(
        kernel,
        out_shape=jax.ShapeDtypeStruct(terms.shape[1:], F32),
        in_specs=[VMEM],
        out_specs=VMEM,
        scratch_shapes=line_scratch(parts, terms),
        compiler_params=params(collective_id),
        name=name,
    )(terms)


def last_exchange(parts, groups, partial, terms):
    block = terms.shape[1:]

    def kernel(
        partial_in, terms_in, partial_out, sums_out, land, total, send, recv,
        sum_send, sum_recv, own, *line_refs
    ):
        dp = lax.axis_index("dp")
        greet((("seq", parts), ("dp", groups)))
        dp_copies = []
        for step in range(1, groups):
            target = lax.rem(dp + step, groups)
            copy = remote(
                terms_in.at[target], land.at[dp], send.at[step], recv.at[step], "dp", target
            )
            copy.start()
            dp_copies.append(copy)
        line = line_reduce(parts, partial_in, partial_out, *line_refs)
        next(line)
        for copy in dp_copies:
            copy.wait()
        summed = terms_in[dp].astype(F32)
        for step in range(1, groups):
            summed = summed + land[lax.rem(dp + step, groups)].astype(F32)
        total[...] = summed.astype(LOW)
        sums = line_gather(parts, total, sums_out, sum_send, sum_recv, own)
        next(sums)
        run(sums, line)

    dma = pltpu.SemaphoreType.DMA
    return pl.pallas_call(
        kernel,
        out_shape=[
            jax.ShapeDtypeStruct(partial.shape[1:], F32),
            jax.ShapeDtypeStruct((parts,) + block, terms.dtype),
        ],
        in_specs=[VMEM, VMEM],
        out_specs=[VMEM, ANY],
        scratch_shapes=[
            pltpu.VMEM(terms.shape, terms.dtype),
            pltpu.VMEM(block, terms.dtype),
            dma((groups,)),
            dma((groups,)),
            dma((2, parts)),
            dma((2, parts)),
            dma,
        ]
        + line_scratch(parts, partial),
        compiler_params=params(4),
        name="last_exchange",
    )(partial, terms)


def norm_reduce(parts, groups, terms):
    block = terms.shape[1:]

    def kernel(terms_in, out, land, total, seq_land, send, recv, seq_send, seq_recv):
        seq, dp = lax.axis_index("seq"), lax.axis_index("dp")
        greet((("seq", parts), ("dp", groups)))
        copies = []
        for step in range(1, groups):
            target = lax.rem(dp + step, groups)
            copy = remote(
                terms_in.at[target], land.at[dp], send.at[step], recv.at[step], "dp", target
            )
            copy.start()
            copies.append(copy)
        for copy in copies:
            copy.wait()
        summed = terms_in[dp]
        for step in range(1, groups):
            summed = summed + land[lax.rem(dp + step, groups)]
        total[...] = summed
        copies = []
        for step in range(1, parts):
            copy = remote(
                total,
                seq_land.at[seq],
                seq_send.at[step],
                seq_recv.at[step],
                "seq",
                lax.rem(seq + step, parts),
            )
            copy.start()
            copies.append(copy)
        for copy in copies:
            copy.wait()
        for step in range(1, parts):
            summed = summed + seq_land[lax.rem(seq + step, parts)]
        out[...] = summed

    dma = pltpu.SemaphoreType.DMA
    return pl.pallas_call(
        kernel,
        out_shape=jax.ShapeDtypeStruct(block, terms.dtype),
        in_specs=[VMEM],
        out_specs=VMEM,
        scratch_shapes=[
            pltpu.VMEM(terms.shape, terms.dtype),
            pltpu.VMEM(block, terms.dtype),
            pltpu.VMEM((parts,) + block, terms.dtype),
            dma((groups,)),
            dma((groups,)),
            dma((parts,)),
            dma((parts,)),
        ],
        compiler_params=params(5),
        name="norm_reduce",
    )(terms)


def attention_forward(queries, keys, values):
    length, local_width = queries.shape
    heads_here = local_width // HEAD_DIM
    block_rows = min(512, length)
    blocks = length // block_rows
    scale = HEAD_DIM ** (-0.5)
    outs, logs = [], []
    key_index = jnp.arange(length)
    for b in range(blocks):
        seen = (b + 1) * block_rows
        q = queries[b * block_rows : seen].reshape(block_rows, heads_here, HEAD_DIM)
        k = keys[:seen].reshape(seen, heads_here, HEAD_DIM)
        v = values[:seen].reshape(seen, heads_here, HEAD_DIM)
        raw = jnp.einsum("qhd,khd->hqk", q, k, preferred_element_type=F32)
        positions = b * block_rows + jnp.arange(block_rows)
        causal = key_index[None, :seen] <= positions[:, None]
        scores = jnp.where(causal[None], raw * scale, -1e30)
        largest = jnp.max(scores, -1, keepdims=True)
        expo = jnp.exp(scores - largest)
        total = jnp.sum(expo, -1, keepdims=True)
        probs = (expo / total).astype(LOW)
        context = jnp.einsum("hqk,khd->qhd", probs, v, preferred_element_type=F32)
        outs.append(context.astype(LOW).reshape(block_rows, local_width))
        logs.append(largest + jnp.log(total))
    return jnp.concatenate(outs, axis=0), logs


def attention_backward(queries, keys, values, grads, logs):
    length, local_width = queries.shape
    heads_here = local_width // HEAD_DIM
    block_rows = min(512, length)
    blocks = length // block_rows
    scale = HEAD_DIM ** (-0.5)
    key_index = jnp.arange(length)
    query_grads = []
    key_sum = jnp.zeros((length, heads_here, HEAD_DIM), F32)
    value_sum = jnp.zeros((length, heads_here, HEAD_DIM), F32)
    for b in range(blocks):
        seen = (b + 1) * block_rows
        q = queries[b * block_rows : seen].reshape(block_rows, heads_here, HEAD_DIM)
        g = grads[b * block_rows : seen].reshape(block_rows, heads_here, HEAD_DIM)
        k = keys[:seen].reshape(seen, heads_here, HEAD_DIM)
        v = values[:seen].reshape(seen, heads_here, HEAD_DIM)
        raw = jnp.einsum("qhd,khd->hqk", q, k, preferred_element_type=F32)
        positions = b * block_rows + jnp.arange(block_rows)
        causal = key_index[None, :seen] <= positions[:, None]
        scores = jnp.where(causal[None], raw * scale, -1e30)
        probs = jnp.exp(scores - logs[b])
        low_probs = probs.astype(LOW)
        value_term = jnp.einsum("hqk,qhd->khd", low_probs, g, preferred_element_type=F32)
        prob_grad = jnp.einsum("qhd,khd->hqk", g, v, preferred_element_type=F32)
        score_grad = (
            probs * (prob_grad - jnp.sum(probs * prob_grad, -1, keepdims=True))
        ).astype(LOW)
        query_grad = jnp.einsum("hqk,khd->qhd", score_grad, k, preferred_element_type=F32) * scale
        key_term = jnp.einsum("hqk,qhd->khd", score_grad, q, preferred_element_type=F32) * scale
        pad = ((0, length - seen), (0, 0), (0, 0))
        key_sum = key_sum + jnp.pad(key_term, pad)
        value_sum = value_sum + jnp.pad(value_term, pad)
        query_grads.append(query_grad.astype(LOW).reshape(block_rows, local_width))
    return (
        jnp.concatenate(query_grads, axis=0),
        key_sum.astype(LOW).reshape(length, local_width),
        value_sum.astype(LOW).reshape(length, local_width),
    )


def on_device(
    tokens,
    qkv_weight,
    proj_weight,
    hidden_weight,
    output_weight,
    first_gain,
    first_bias,
    second_gain,
    second_bias,
    cotangent,
):
    parts = lax.axis_size("seq")
    groups = lax.axis_size("dp")
    part = lax.axis_index("seq")
    inputs_low = tokens[0]
    rows, width = inputs_low.shape
    model_rows = qkv_weight.shape[0]
    local_width = width // parts
    hidden_rows = output_weight.shape[0] // parts
    hidden_here = hidden_rows * groups

    qkv_here = lax.dynamic_index_in_dim(
        qkv_weight.reshape(model_rows, 3, parts, local_width), part, 2, keepdims=False
    ).reshape(model_rows, 3 * local_width)
    hidden_cols = lax.dynamic_index_in_dim(
        hidden_weight.reshape(model_rows, groups, parts, hidden_rows), part, 2, keepdims=False
    ).reshape(model_rows, hidden_here)
    output_here = lax.dynamic_slice_in_dim(output_weight, part * hidden_rows, hidden_rows, 0)
    direct = model_rows % 16 == 0 and rows % 16 == 0 and groups % 2 == 0
    norms = jnp.stack([first_gain, first_bias, second_gain, second_bias], axis=0)
    if direct:
        pad_lanes = -first_gain.shape[0] % 128
        padded = jnp.pad(norms.astype(F32), ((0, 4), (0, pad_lanes)))
        all_tokens, *pieces = start_gather(
            parts,
            groups,
            inputs_low,
            (qkv_here, padded, proj_weight, hidden_cols, output_here),
        )
        wide_qkv, wide_proj, wide_hidden, wide_output = [
            pieces[at].reshape(groups * pieces[at].shape[1], pieces[at].shape[2])
            for at in (0, 2, 3, 4)
        ]
        norms = pieces[1][:, :4, : first_gain.shape[0]].transpose(1, 0, 2).reshape(4, width)
        all_tokens = all_tokens.reshape(parts * rows, width)
        own_grads, all_tokens = lax.optimization_barrier((cotangent[0], all_tokens))
        all_grads = gather_seq(own_grads)
    else:
        norms = lax.all_gather(norms, "dp", axis=1, tiled=True).astype(F32)
        all_tokens = gather_seq(inputs_low)
        wide_qkv = lax.all_gather(qkv_here, "dp", axis=0, tiled=True)
        wide_proj = lax.all_gather(proj_weight, "dp", axis=0, tiled=True)
        wide_hidden = lax.all_gather(hidden_cols, "dp", axis=0, tiled=True)
        wide_output = lax.all_gather(output_here, "dp", axis=0, tiled=True)
        all_grads = gather_seq(cotangent[0])
    gain_one, bias_one, gain_two, bias_two = norms[0], norms[1], norms[2], norms[3]

    inputs = all_tokens.astype(F32)
    lowered_one = layer_norm(inputs, gain_one, bias_one).astype(LOW)
    projected = matmul(lowered_one, wide_qkv).astype(LOW)
    queries = projected[:, :local_width]
    keys = projected[:, local_width : 2 * local_width]
    values = projected[:, 2 * local_width :]
    context_here, logs = attention_forward(queries, keys, values)
    if direct:
        half = context_here.shape[0] // 2
        folded = jnp.concatenate([context_here[:half], context_here[half:]], axis=1)
        context = seq_gather(parts, folded, 1, "context_gather")
        context = context.reshape(parts, half, 2, local_width).transpose(2, 1, 0, 3)
        context = context.reshape(parts * rows, width)
    else:
        context = lax.all_gather(context_here, "seq", axis=1, tiled=True)
    middle = inputs + matmul(context, wide_proj)
    lowered_two = layer_norm(middle, gain_two, bias_two).astype(LOW)
    hidden_pre = matmul(lowered_two, wide_hidden)
    activated_float, gelu_pull = jax.vjp(gelu_tanh, hidden_pre)
    activated = activated_float.astype(LOW)

    act_grad = matmul_right_t(all_grads, wide_output)
    pre_grad = gelu_pull(act_grad)[0].astype(LOW)
    normed_two_grad = matmul_right_t(pre_grad, wide_hidden)
    if direct:
        normed_two_grad = seq_reduce(
            parts,
            normed_two_grad.astype(LOW).reshape(parts, rows, width),
            2,
            "hidden_reduce",
        )
    else:
        normed_two_grad = scatter_seq(normed_two_grad)
    middle_own = lax.dynamic_slice_in_dim(middle, part * rows, rows, 0)
    _, norm_pull_two = jax.vjp(layer_norm, middle_own, gain_two, bias_two)
    middle_part, gain_two_term, bias_two_term = norm_pull_two(normed_two_grad)
    middle_grad = cotangent[0].astype(F32) + middle_part
    if direct:
        attn_grad = seq_gather(parts, middle_grad.astype(LOW), 3, "attn_gather")
        attn_grad = attn_grad.reshape(parts * rows, width)
    else:
        attn_grad = gather_seq(middle_grad.astype(LOW))

    ffn_terms = matmul(activated, wide_output).astype(LOW)
    ffn_terms, attn_grad = lax.optimization_barrier((ffn_terms, attn_grad))
    block_out = middle_own + scatter_seq(ffn_terms)
    proj_here = lax.dynamic_slice_in_dim(wide_proj, part * local_width, local_width, 0)
    context_grad = matmul_right_t(attn_grad, proj_here).astype(LOW)
    query_grads, key_grads, value_grads = attention_backward(
        queries, keys, values, context_grad, logs
    )
    qkv_grad = jnp.concatenate([query_grads, key_grads, value_grads], axis=1)
    attn_cols = lax.dynamic_slice_in_dim(attn_grad, part * local_width, local_width, 1)
    proj_term = matmul_left_t(context, attn_cols).astype(LOW)
    qkv_term = matmul_left_t(lowered_one, qkv_grad).astype(LOW)
    second_terms = jnp.concatenate([proj_term, qkv_term], axis=1)
    normed_one_grad = matmul_right_t(qkv_grad, wide_qkv)
    if direct:
        normed_one_grad, second_all = last_exchange(
            parts,
            groups,
            normed_one_grad.astype(LOW).reshape(parts, rows, width),
            second_terms.reshape(groups, model_rows, second_terms.shape[1]),
        )
    else:
        normed_one_grad = scatter_seq(normed_one_grad)
        second_sum = lax.psum_scatter(second_terms, "dp", scatter_dimension=0, tiled=True)
        second_all = lax.all_gather(second_sum, "seq", axis=0)
    _, norm_pull_one = jax.vjp(layer_norm, inputs_low.astype(F32), gain_one, bias_one)
    input_part, gain_one_term, bias_one_term = norm_pull_one(normed_one_grad)
    tokens_gradient = (middle_grad + input_part).astype(LOW)

    output_term = matmul_left_t(activated, all_grads).astype(LOW)
    hidden_term = matmul_left_t(lowered_two, pre_grad).astype(LOW)
    first_terms = jnp.concatenate([output_term, hidden_term], axis=1)
    first_sum = lax.psum_scatter(first_terms, "dp", scatter_dimension=0, tiled=True)
    first_all = lax.all_gather(first_sum, "seq", axis=0)
    output_gradient = first_all[:, :, :width].reshape(parts * hidden_rows, width).astype(F32)
    hidden_gradient = (
        first_all[:, :, width:]
        .reshape(parts, model_rows, groups, hidden_rows)
        .transpose(1, 2, 0, 3)
        .reshape(model_rows, parts * hidden_here)
        .astype(F32)
    )
    proj_gradient = (
        second_all[:, :, :local_width].transpose(1, 0, 2).reshape(model_rows, width).astype(F32)
    )
    qkv_gradient = (
        second_all[:, :, local_width:]
        .reshape(parts, model_rows, 3, local_width)
        .transpose(1, 2, 0, 3)
        .reshape(model_rows, 3 * width)
        .astype(F32)
    )
    norm_terms = jnp.stack([gain_one_term, bias_one_term, gain_two_term, bias_two_term], axis=0)
    if direct:
        norm_blocks = norm_terms.reshape(4, groups, model_rows).transpose(1, 0, 2)
        norm_blocks = jnp.pad(norm_blocks, ((0, 0), (0, 4), (0, -model_rows % 128)))
        norm_own = norm_reduce(parts, groups, norm_blocks)[:4, :model_rows]
    else:
        norm_sum = lax.psum(norm_terms, ("seq", "dp"))
        norm_own = lax.dynamic_slice_in_dim(
            norm_sum, lax.axis_index("dp") * model_rows, model_rows, 1
        )
    return (
        block_out.astype(LOW)[None],
        tokens_gradient[None],
        qkv_gradient,
        proj_gradient,
        hidden_gradient,
        output_gradient,
        norm_own[0],
        norm_own[1],
        norm_own[2],
        norm_own[3],
    )


def solution(mesh):
    placed = (
        P("dp", "seq", None),
        P("dp", None),
        P("dp", None),
        P("dp", None),
        P("dp", None),
        P("dp"),
        P("dp"),
        P("dp"),
        P("dp"),
        P("dp", "seq", None),
    )
    return jax.shard_map(
        on_device,
        mesh=mesh,
        in_specs=placed,
        out_specs=(
            P("dp", "seq", None),
            P("dp", "seq", None),
            P("dp", None),
            P("dp", None),
            P("dp", None),
            P("dp", None),
            P("dp"),
            P("dp"),
            P("dp"),
            P("dp"),
        ),
        check_vma=False,
    )
```

profile of v0, /device:TPU:0, one launch (start us, length us, event | category | flops | bytes accessed | tf_op | source)
XLA Modules:
  0.0 362.8 jit_solution(7841313083405965475)
XLA Ops:
  7.3 1.7 reshape.301
  9.7 2.3 reshape.303
  12.0 1.2 dynamic-slice_reduce_fusion.1
  13.6 53.9 %start_gather.1 = (bf16[4,256,768]{2,1,0:T(8,128)(2,1)S(1)}, bf16[8,96,576]{2,1,0:T(8,128)(2,1)S(1)}, f32[8,8,128]{2,1,0:T(8,128)S(1)}, bf16[8,96,768]{2,1,0:T(8...) custom-call(bf16[256,768]{1,0:T(8,128)(2,1)S(1)} %bitcast.136, ...), custom_call_target="tpu_custom_call" | custom-call | tf_op jit(solution)/shard_map/start_gather/pallas_call | solution.py:278
  73.1 1.4 convolution_convert_fusion.5
  78.7 1.8 fusion.86
  81.0 1.3 fusion.43
  83.4 1.4 fusion.85
  84.9 1.5 fusion
  86.4 1.2 copy-done.15
  87.6 1.7 fusion.44
  89.5 43.8 %context_gather.1 = bf16[4,512,384]{2,1,0:T(8,128)(2,1)S(1)} custom-call(bf16[512,384]{1,0:T(8,128)(2,1)S(1)} %pad_maximum_fusion.3.in_ref), custom_call_target="tpu_custom_call" | custom-call | tf_op jit(solution)/shard_map/context_gather/pallas_call | solution.py:303
  134.5 3.1 copy.74
  137.6 3.0 copy.75
  140.6 1.6 copy.95
  142.2 3.4 fusion.87
  147.7 1.7 add_convert_fusion
  149.4 3.3 fusion.88
  152.7 2.9 fusion.14
  155.7 1.5 convolution_convert_fusion.3
  157.2 1.4 convolution_convert_fusion.1
  158.6 29.5 %hidden_reduce.1 = f32[256,768]{1,0:T(8,128)S(1)} custom-call(bf16[4,256,768]{2,1,0:T(8,128)(2,1)S(1)} %bitcast.145), custom_call_target="tpu_custom_call" | custom-call | tf_op jit(solution)/shard_map/hidden_reduce/pallas_call | solution.py:332
  188.1 1.7 convolution_convert_fusion.4
  189.8 1.6 pad_maximum_fusion
  191.4 4.3 %copy.91 = bf16[768,1536]{1,0:T(8,128)(2,1)} copy(bf16[768,1536]{0,1:T(8,128)(2,1)} %pad_maximum_fusion) | data formatting | bytes 4718592
  195.8 1.4 multiply_reduce_fusion.3
  198.6 1.6 fusion.80
  202.2 26.6 %attn_gather.1 = bf16[4,256,768]{2,1,0:T(8,128)(2,1)S(1)} custom-call(bf16[256,768]{1,0:T(8,128)(2,1)S(1)} %fusion.54.in_ref), custom_call_target="tpu_custom_call" | custom-call | tf_op jit(solution)/shard_map/attn_gather/pallas_call | solution.py:303
  230.0 3.2 convolution_convert_fusion.2
  233.2 2.2 convolution_convert_fusion.7
  235.5 3.2 convolution_convert_fusion.8
  241.3 1.3 fusion.40
  243.0 3.9 %multiply_reduce_fusion = (f32[3,512]{1,0:T(4,128)S(1)}, f32[3,512,1024]{2,1,0:T(8,128)S(1)}) fusion(f32[3,512,1024]{2,1,0:T(8,128)} %copy-done.15, f32[3,512]{1,0:T(4,128)S(1)} %log_add_fusion, bf16[512,3,64]{0,2,1:T(8,128)(2,1)S(1)} %bitcast.174, bf16[1024,3,64]{0,2,1:T(8,128)(2,1)S(1)} %bitcast.177), kind=kOutput, calls=%fused_computation.1 | convolution fusion | flops 206043648 | bytes 13185024 | tf_op jit(solution)/shard_map/qhd,khd->hqk/dot_general | solution.py:504
  247.7 1.4 multiply_convert_fusion
  254.1 1.3 convolution_convert_fusion.6
  256.5 2.4 copy.80
  258.9 2.5 convolution_convert_fusion
  261.5 53.9 %last_exchange.1 = (f32[256,768]{1,0:T(8,128)S(1)}, bf16[4,96,768]{2,1,0:T(8,128)(2,1)S(1)}) custom-call(bf16[4,256,768]{2,1,0:T(8,128)(2,1)S(1)} %bitcast.146, bf16[8,96,768]{2,1,0:T(8,128)(2,1)S(1)} %bitcast.142), custom_call_target="tpu_custom_call" | custom-call | tf_op jit(solution)/shard_map/last_exchange/pallas_call | solution.py:373
  316.5 9.5 %norm_reduce.1 = f32[8,128]{1,0:T(8,128)S(1)} custom-call(f32[8,8,128]{2,1,0:T(8,128)S(1)} %pad.21.terms_in), custom_call_target="tpu_custom_call" | custom-call | tf_op jit(solution)/shard_map/norm_reduce/pallas_call | solution.py:435
  328.4 2.7 copy.81
  331.1 2.5 copy.82
  333.6 2.9 reshape.330
  338.2 2.1 fusion.55
  340.3 4.4 %all-gather.6.cloned.1.call-done = bf16[384,1536]{1,0:T(8,128)(2,1)} async-done(((bf16[96,1536]{1,0:T(8,128)(2,1)}), bf16[384,1536]{1,0:T(8,128)(2,1)}) %all-gather.6.cloned.1.call-update) | async-done | bytes 1179664 | tf_op jit(solution)/shard_map/all_gather | solution.py:655
  344.7 2.4 fusion.81
  348.2 2.0 reshape.335
  350.2 2.2 copy.85
  352.4 3.6 reshape.332
  (206 shorter events, 36.2 us)
Async XLA Ops:
  7.2 6.3 %copy-start = (bf16[384,768]{1,0:T(8,128)(2,1)S(1)}, bf16[384,768]{1,0:T(8,128)(2,1)}, u32[]{:S(2)}) copy-start(bf16[384,768]{1,0:T(8,128)(2,1)} %param.14) | copy-start | bytes 1769476
  7.2 6.3 %copy-start.55 = (bf16[96]{0:T(256)(128)(2,1)S(1)}, bf16[96]{0:T(256)(128)(2,1)}, u32[]{:S(2)}) copy-start(bf16[96]{0:T(256)(128)(2,1)} %param.18) | copy-start | bytes 580
  7.2 6.3 %copy-start.56 = (bf16[96]{0:T(256)(128)(2,1)S(1)}, bf16[96]{0:T(256)(128)(2,1)}, u32[]{:S(2)}) copy-start(bf16[96]{0:T(256)(128)(2,1)} %param.17) | copy-start | bytes 580
  7.2 6.3 %copy-start.57 = (bf16[96]{0:T(256)(128)(2,1)S(1)}, bf16[96]{0:T(256)(128)(2,1)}, u32[]{:S(2)}) copy-start(bf16[96]{0:T(256)(128)(2,1)} %param.16) | copy-start | bytes 580
  7.2 6.3 %copy-start.58 = (bf16[96]{0:T(256)(128)(2,1)S(1)}, bf16[96]{0:T(256)(128)(2,1)}, u32[]{:S(2)}) copy-start(bf16[96]{0:T(256)(128)(2,1)} %param.15) | copy-start | bytes 580
  7.2 6.3 %copy-start.2 = (bf16[1,256,768]{2,1,0:T(8,128)(2,1)S(1)}, bf16[1,256,768]{2,1,0:T(8,128)(2,1)}, u32[]{:S(2)}) copy-start(bf16[1,256,768]{2,1,0:T(8,128)(2,1)} %param.10) | copy-start | bytes 1179652
  7.2 6.3 %copy-start.6 = (bf16[96,768]{1,0:T(8,128)(2,1)S(1)}, bf16[96,768]{1,0:T(8,128)(2,1)}, u32[]{:S(2)}) copy-start(bf16[96,768]{1,0:T(8,128)(2,1)} %refs_3_.1) | copy-start | bytes 442372
  7.3 142.1 %all-gather.4.cloned.1.call-start = ((), (), s32[]{:S(2)}) async-start(), calls=%async_computation.2 | async-start | bytes 1966080 | tf_op jit(solution)/shard_map/all_gather | solution.py:37
  71.6 1.5 copy-start.13
  71.6 244.2 %reduce-scatter.7.cloned.1.call-start = ((), (), s32[]{:S(2)}) async-start(), calls=%async_computation.5 | async-start | bytes 2654208 | tf_op jit(solution)/shard_map/reduce_scatter | solution.py:654
  72.2 2.3 copy-start.44
  72.8 1.7 copy-start.51
  73.0 1.5 copy-start.38
  75.3 5.7 %copy-start.25 = (bf16[512,192]{0,1:T(8,128)(2,1)}, bf16[512,192]{0,1:T(8,128)(2,1)S(1)}, u32[]{:S(2)}) copy-start(bf16[512,192]{0,1:T(8,128)(2,1)S(1)} %get-tuple-element.50) | copy-start | bytes 589828
  76.1 7.3 %copy-start.22 = (bf16[1024,192]{0,1:T(8,128)(2,1)}, bf16[1024,192]{0,1:T(8,128)(2,1)S(1)}, u32[]{:S(2)}) copy-start(bf16[1024,192]{0,1:T(8,128)(2,1)S(1)} %get-tuple-element.54) | copy-start | bytes 1179652
  78.7 2.2 copy-start.32
  80.5 1.8 copy-start.16
  84.8 2.7 copy-start.15
  84.8 2.7 copy-start.36
  84.9 2.7 copy-start.27
  145.6 2.1 copy-start.19
  145.6 2.0 copy-start.42
  145.6 2.1 copy-start.37
  145.6 2.1 copy-start.40
  145.6 2.1 copy-start.46
  149.4 3.3 copy-start.11
  149.4 3.3 copy-start.29
  155.7 32.4 %copy-start.60 = (f32[1024,768]{1,0:T(8,128)}, f32[1024,768]{1,0:T(8,128)S(1)}, u32[]{:S(2)}) copy-start(f32[1024,768]{1,0:T(8,128)S(1)} %get-tuple-element.71) | copy-start | bytes 9437188
  157.2 30.9 %copy-start.59 = (bf16[1024,768]{1,0:T(8,128)(2,1)S(1)}, bf16[1024,768]{1,0:T(8,128)(2,1)}, u32[]{:S(2)}) copy-start(bf16[1024,768]{1,0:T(8,128)(2,1)} %all-gather.4.cloned.1.call-done) | copy-start | bytes 4718596
  195.7 142.5 %reduce-scatter.5.cloned.1.call-start = ((), (), s32[]{:S(2)}) async-start(), calls=%async_computation.3 | async-start | bytes 1966080 | tf_op jit(solution)/shard_map/reduce_scatter | solution.py:41
  198.5 31.5 %copy-start.9 = (bf16[8,96,768]{2,1,0:T(8,128)(2,1)S(1)}, bf16[8,96,768]{2,1,0:T(8,128)(2,1)}, u32[]{:S(2)}) copy-start(bf16[8,96,768]{2,1,0:T(8,128)(2,1)} %copy-done.8) | copy-start | bytes 3538948
  198.5 31.5 %copy-start.61 = (f32[1024,768]{1,0:T(8,128)S(1)}, f32[1024,768]{1,0:T(8,128)}, u32[]{:S(2)}) copy-start(f32[1024,768]{1,0:T(8,128)} %copy-done.60) | copy-start | bytes 9437188
  233.2 5.5 %copy-start.33 = (bf16[512,192]{0,1:T(8,128)(2,1)S(1)}, bf16[512,192]{0,1:T(8,128)(2,1)}, u32[]{:S(2)}) copy-start(bf16[512,192]{0,1:T(8,128)(2,1)} %get-tuple-element.53) | copy-start | bytes 589828
  233.2 5.5 %copy-start.17 = (f32[3,512,512]{1,2,0:T(8,128)S(1)}, f32[3,512,512]{1,2,0:T(8,128)}, u32[]{:S(2)}) copy-start(f32[3,512,512]{1,2,0:T(8,128)} %copy-done.16) | copy-start | bytes 9437188
  240.3 2.7 copy-start.28
  242.7 102.0 %all-gather.6.cloned.1.call-start = ((), (), s32[]{:S(2)}) async-start(), calls=%async_computation.4 | async-start | bytes 1474560 | tf_op jit(solution)/shard_map/all_gather | solution.py:655
  243.0 4.0 %slice-start = ((s8[6291456]{0:T(1024)(128)(4,1)}), s8[4194304]{0:T(1024)(128)(4,1)S(1)}, s32[]{:S(2)}) async-start(s8[6291456]{0:T(1024)(128)(4,1)} %bitcast.155), calls=%async_computation.6 | async-start | bytes 8388608
  243.0 4.7 %slice-start.1 = ((s8[6291456]{0:T(1024)(128)(4,1)}), s8[2097152]{0:T(1024)(128)(4,1)S(1)}, s32[]{:S(2)}) async-start(s8[6291456]{0:T(1024)(128)(4,1)} %bitcast.155), calls=%async_computation.7 | async-start | bytes 4194304
  250.2 1.9 copy-start.18
  255.4 3.5 copy-start.14
  258.9 2.6 copy-start.4
  258.9 56.5 %copy-start.43 = (f32[256]{0:T(256)S(1)}, f32[256]{0:T(256)}, u32[]{:S(2)}) copy-start(f32[256]{0:T(256)} %broadcast_multiply_fusion.2) | copy-start | bytes 3076
  261.5 55.0 %copy-start.47 = (f32[1,8,96]{2,0,1:T(1,128)S(1)}, f32[1,8,96]{2,0,1:T(1,128)}, u32[]{:S(2)}) copy-start(f32[1,8,96]{2,0,1:T(1,128)} %stack.37) | copy-start | bytes 9220
  261.5 55.0 %copy-start.48 = (f32[1,8,96]{2,0,1:T(1,128)S(1)}, f32[1,8,96]{2,0,1:T(1,128)}, u32[]{:S(2)}) copy-start(f32[1,8,96]{2,0,1:T(1,128)} %stack.38) | copy-start | bytes 9220
  328.4 8.7 %copy-start.21 = (f32[256,768]{1,0:T(8,128)S(1)}, f32[256,768]{1,0:T(8,128)}, u32[]{:S(2)}) copy-start(f32[256,768]{1,0:T(8,128)} %copy-done.20) | copy-start | bytes 2359300
  328.4 8.7 %copy-start.24 = (bf16[1,256,768]{2,1,0:T(8,128)(2,1)S(1)}, bf16[1,256,768]{2,1,0:T(8,128)(2,1)}, u32[]{:S(2)}) copy-start(bf16[1,256,768]{2,1,0:T(8,128)(2,1)} %param.19) | copy-start | bytes 1179652
  328.4 8.7 %copy-start.50 = (f32[256]{0:T(256)S(1)}, f32[256]{0:T(256)}, u32[]{:S(2)}) copy-start(f32[256]{0:T(256)} %copy-done.49) | copy-start | bytes 3076
  348.2 7.8 %copy-start.1 = (bf16[384,768]{1,0:T(8,128)(2,1)S(1)}, bf16[384,768]{1,0:T(8,128)(2,1)}, u32[]{:S(2)}) copy-start(bf16[384,768]{1,0:T(8,128)(2,1)} %param.14) | copy-start | bytes 1769476
  (20 other events, 23.4 us)
Sparse Core Ops, SparseCore 0:
  71.7 42.1 all-gather.3
  195.8 41.7 reduce-scatter.6
  242.8 43.4 reduce-scatter.4
  315.9 28.7 all-gather.5
where the time goes:
time: 367 us; the launch traced here: 363 us
  Pallas kernels  217 us (59%)
  local copies, waits for them, and re-layouts  54.6 us (15%)
  matrix products  45 us (12%)
  other arithmetic  25.8 us (7%)
  between operations  15.1 us (4%)
  waiting for transfers between devices  4.52 us (1%)
    pallas_call x2, Pallas kernels, seq_gather(): pl.pallas_call(kernel, out_shape=jax.ShapeDtypeStruct((parts,) + value.sh...  70.4 us
    pallas_call x1, Pallas kernels, start_gather(): pl.pallas_call(kernel, out_shape=[jax.ShapeDtypeStruct((parts,) + tokens....  53.9 us
    pallas_call x1, Pallas kernels, last_exchange(): pl.pallas_call(kernel, out_shape=[jax.ShapeDtypeStruct(partial.shape[1:],...  53.9 us
    pallas_call x1, Pallas kernels, seq_reduce(): pl.pallas_call(kernel, out_shape=jax.ShapeDtypeStruct(terms.shape[1:], F3...  29.5 us
    unnamed x131, local copies, waits for them, and re-layouts  16.8 us
    dot_general x4, matrix products, matmul(): return jnp.dot(left, right, preferred_element_type=F32)  10.8 us
    dot_general x4, matrix products, matmul_right_t(): lax.dot_general(left, right, (((1,), (1,)), ((), ())), preferred_element_...  9.53 us
    pallas_call x1, Pallas kernels, norm_reduce(): pl.pallas_call(kernel, out_shape=jax.ShapeDtypeStruct(block, terms.dtype)...  9.47 us
  transfers between devices with their start and end apart: 4, of which 1 were waited for; matrix products, arithmetic and copies ran while one was open for 22% of the time, Pallas kernels for 37%

commit v1 on v0

--- a/solution.py
+++ b/solution.py
@@ -256,6 +256,7 @@
             copy = pltpu.make_async_copy(piece_in[k], piece_out[k].at[dp], own.at[k])
             copy.start()
             local.append(copy)
+        next(line)
         for k, step, copy in far:
             copy.wait_recv()
             origin = lax.rem(dp - 2 * step + groups, groups)

time: 367 us -> 351 us (0.956)
  Pallas kernels: 217 us -> 201 us
    pallas_call x1, Pallas kernels: 53.9 us -> 39.7 us  [start_gather(): pl.pallas_call(kernel, out_shape=[jax.ShapeDtypeStruct((parts,) + tokens....]
  transfers between devices with their start and end apart: 4 -> 4, of which waited for: 1 -> 1; matrix products, arithmetic and copies ran while one was open for 22% -> 23% of each run, Pallas kernels for 37% -> 38%
where the time goes in v1:
time: 351 us; the launch traced here: 347 us
  Pallas kernels  201 us (57%)
  local copies, waits for them, and re-layouts  54.6 us (16%)
  matrix products  44.9 us (13%)
  other arithmetic  25.8 us (7%)
  between operations  15.1 us (4%)
  waiting for transfers between devices  4.52 us (1%)
    pallas_call x2, Pallas kernels, seq_gather(): pl.pallas_call(kernel, out_shape=jax.ShapeDtypeStruct((parts,) + value.sh...  68.7 us
    pallas_call x1, Pallas kernels, last_exchange(): pl.pallas_call(kernel, out_shape=[jax.ShapeDtypeStruct(partial.shape[1:],...  55.8 us
    pallas_call x1, Pallas kernels, start_gather(): pl.pallas_call(kernel, out_shape=[jax.ShapeDtypeStruct((parts,) + tokens....  39.7 us
    pallas_call x1, Pallas kernels, seq_reduce(): pl.pallas_call(kernel, out_shape=jax.ShapeDtypeStruct(terms.shape[1:], F3...  28.1 us
    unnamed x131, local copies, waits for them, and re-layouts  16.7 us
    dot_general x4, matrix products, matmul(): return jnp.dot(left, right, preferred_element_type=F32)  10.8 us
    dot_general x4, matrix products, matmul_right_t(): lax.dot_general(left, right, (((1,), (1,)), ((), ())), preferred_element_...  9.53 us
    pallas_call x1, Pallas kernels, norm_reduce(): pl.pallas_call(kernel, out_shape=jax.ShapeDtypeStruct(block, terms.dtype)...  8.83 us
  transfers between devices with their start and end apart: 4, of which 1 were waited for; matrix products, arithmetic and copies ran while one was open for 23% of the time, Pallas kernels for 38%

profile of v1, /device:TPU:0, one launch (start us, length us, event | category | flops | bytes accessed | tf_op | source)
XLA Modules:
  0.0 346.8 jit_solution(12689860525513701155)
XLA Ops:
  7.3 1.7 reshape.301
  9.7 2.3 reshape.303
  12.0 1.2 dynamic-slice_reduce_fusion.1
  13.6 39.7 %start_gather.1 = (bf16[4,256,768]{2,1,0:T(8,128)(2,1)S(1)}, bf16[8,96,576]{2,1,0:T(8,128)(2,1)S(1)}, f32[8,8,128]{2,1,0:T(8,128)S(1)}, bf16[8,96,768]{2,1,0:T(8...) custom-call(bf16[256,768]{1,0:T(8,128)(2,1)S(1)} %bitcast.136, ...), custom_call_target="tpu_custom_call" | custom-call | tf_op jit(solution)/shard_map/start_gather/pallas_call | solution.py:279
  58.9 1.4 convolution_convert_fusion.5
  64.5 1.8 fusion.86
  66.8 1.3 fusion.43
  69.2 1.4 fusion.85
  70.7 1.5 fusion
  72.2 1.2 copy-done.15
  73.4 1.7 fusion.44
  75.4 42.9 %context_gather.1 = bf16[4,512,384]{2,1,0:T(8,128)(2,1)S(1)} custom-call(bf16[512,384]{1,0:T(8,128)(2,1)S(1)} %pad_maximum_fusion.3.in_ref), custom_call_target="tpu_custom_call" | custom-call | tf_op jit(solution)/shard_map/context_gather/pallas_call | solution.py:304
  119.5 3.1 copy.74
  122.6 3.0 copy.75
  125.6 1.6 copy.95
  127.2 3.4 fusion.87
  132.6 1.7 add_convert_fusion
  134.3 3.3 fusion.88
  137.7 2.9 fusion.14
  140.6 1.5 convolution_convert_fusion.3
  142.1 1.4 convolution_convert_fusion.1
  143.6 28.1 %hidden_reduce.1 = f32[256,768]{1,0:T(8,128)S(1)} custom-call(bf16[4,256,768]{2,1,0:T(8,128)(2,1)S(1)} %bitcast.145), custom_call_target="tpu_custom_call" | custom-call | tf_op jit(solution)/shard_map/hidden_reduce/pallas_call | solution.py:333
  171.7 1.7 convolution_convert_fusion.4
  173.4 1.6 pad_maximum_fusion
  175.0 4.3 %copy.91 = bf16[768,1536]{1,0:T(8,128)(2,1)} copy(bf16[768,1536]{0,1:T(8,128)(2,1)} %pad_maximum_fusion) | data formatting | bytes 4718592
  179.3 1.4 multiply_reduce_fusion.3
  182.1 1.6 fusion.80
  185.8 25.8 %attn_gather.1 = bf16[4,256,768]{2,1,0:T(8,128)(2,1)S(1)} custom-call(bf16[256,768]{1,0:T(8,128)(2,1)S(1)} %fusion.54.in_ref), custom_call_target="tpu_custom_call" | custom-call | tf_op jit(solution)/shard_map/attn_gather/pallas_call | solution.py:304
  212.8 3.2 convolution_convert_fusion.2
  215.9 2.2 convolution_convert_fusion.7
  218.2 3.2 convolution_convert_fusion.8
  224.1 1.3 fusion.40
  225.8 3.9 %multiply_reduce_fusion = (f32[3,512]{1,0:T(4,128)S(1)}, f32[3,512,1024]{2,1,0:T(8,128)S(1)}) fusion(f32[3,512,1024]{2,1,0:T(8,128)} %copy-done.15, f32[3,512]{1,0:T(4,128)S(1)} %log_add_fusion, bf16[512,3,64]{0,2,1:T(8,128)(2,1)S(1)} %bitcast.174, bf16[1024,3,64]{0,2,1:T(8,128)(2,1)S(1)} %bitcast.177), kind=kOutput, calls=%fused_computation.1 | convolution fusion | flops 206043648 | bytes 13185024 | tf_op jit(solution)/shard_map/qhd,khd->hqk/dot_general | solution.py:505
  230.5 1.4 multiply_convert_fusion
  236.8 1.3 convolution_convert_fusion.6
  239.2 2.4 copy.80
  241.6 2.5 convolution_convert_fusion
  244.2 55.8 %last_exchange.1 = (f32[256,768]{1,0:T(8,128)S(1)}, bf16[4,96,768]{2,1,0:T(8,128)(2,1)S(1)}) custom-call(bf16[4,256,768]{2,1,0:T(8,128)(2,1)S(1)} %bitcast.146, bf16[8,96,768]{2,1,0:T(8,128)(2,1)S(1)} %bitcast.142), custom_call_target="tpu_custom_call" | custom-call | tf_op jit(solution)/shard_map/last_exchange/pallas_call | solution.py:374
  301.1 8.8 %norm_reduce.1 = f32[8,128]{1,0:T(8,128)S(1)} custom-call(f32[8,8,128]{2,1,0:T(8,128)S(1)} %pad.21.terms_in), custom_call_target="tpu_custom_call" | custom-call | tf_op jit(solution)/shard_map/norm_reduce/pallas_call | solution.py:436
  312.4 2.7 copy.81
  315.1 2.5 copy.82
  317.6 2.9 reshape.330
  322.2 2.1 fusion.55
  324.3 4.4 %all-gather.6.cloned.1.call-done = bf16[384,1536]{1,0:T(8,128)(2,1)} async-done(((bf16[96,1536]{1,0:T(8,128)(2,1)}), bf16[384,1536]{1,0:T(8,128)(2,1)}) %all-gather.6.cloned.1.call-update) | async-done | bytes 1179664 | tf_op jit(solution)/shard_map/all_gather | solution.py:656
  328.7 2.4 fusion.81
  332.2 2.0 reshape.335
  334.2 2.2 copy.85
  336.4 3.6 %reshape.332 = f32[96,3072]{1,0:T(8,128)} reshape(f32[96,8,4,96]{3,2,1,0:T(4,128)} %copy.85) | data formatting | bytes 2359296 | tf_op jit(solution)/shard_map/convert_element_type | solution.py:663
  (206 shorter events, 36.2 us)
Async XLA Ops:
  7.2 6.3 %copy-start = (bf16[384,768]{1,0:T(8,128)(2,1)S(1)}, bf16[384,768]{1,0:T(8,128)(2,1)}, u32[]{:S(2)}) copy-start(bf16[384,768]{1,0:T(8,128)(2,1)} %param.14) | copy-start | bytes 1769476
  7.2 6.3 %copy-start.55 = (bf16[96]{0:T(256)(128)(2,1)S(1)}, bf16[96]{0:T(256)(128)(2,1)}, u32[]{:S(2)}) copy-start(bf16[96]{0:T(256)(128)(2,1)} %param.18) | copy-start | bytes 580
  7.2 6.3 %copy-start.56 = (bf16[96]{0:T(256)(128)(2,1)S(1)}, bf16[96]{0:T(256)(128)(2,1)}, u32[]{:S(2)}) copy-start(bf16[96]{0:T(256)(128)(2,1)} %param.17) | copy-start | bytes 580
  7.2 6.3 %copy-start.57 = (bf16[96]{0:T(256)(128)(2,1)S(1)}, bf16[96]{0:T(256)(128)(2,1)}, u32[]{:S(2)}) copy-start(bf16[96]{0:T(256)(128)(2,1)} %param.16) | copy-start | bytes 580
  7.2 6.3 %copy-start.58 = (bf16[96]{0:T(256)(128)(2,1)S(1)}, bf16[96]{0:T(256)(128)(2,1)}, u32[]{:S(2)}) copy-start(bf16[96]{0:T(256)(128)(2,1)} %param.15) | copy-start | bytes 580
  7.2 6.3 %copy-start.2 = (bf16[1,256,768]{2,1,0:T(8,128)(2,1)S(1)}, bf16[1,256,768]{2,1,0:T(8,128)(2,1)}, u32[]{:S(2)}) copy-start(bf16[1,256,768]{2,1,0:T(8,128)(2,1)} %param.10) | copy-start | bytes 1179652
  7.2 6.3 %copy-start.6 = (bf16[96,768]{1,0:T(8,128)(2,1)S(1)}, bf16[96,768]{1,0:T(8,128)(2,1)}, u32[]{:S(2)}) copy-start(bf16[96,768]{1,0:T(8,128)(2,1)} %refs_3_.1) | copy-start | bytes 442372
  7.3 127.1 %all-gather.4.cloned.1.call-start = ((), (), s32[]{:S(2)}) async-start(), calls=%async_computation.2 | async-start | bytes 1966080 | tf_op jit(solution)/shard_map/all_gather | solution.py:37
  57.4 1.5 copy-start.13
  57.4 243.0 %reduce-scatter.7.cloned.1.call-start = ((), (), s32[]{:S(2)}) async-start(), calls=%async_computation.5 | async-start | bytes 2654208 | tf_op jit(solution)/shard_map/reduce_scatter | solution.py:655
  58.0 2.3 copy-start.44
  58.7 1.7 copy-start.51
  58.8 1.5 copy-start.38
  61.1 5.7 %copy-start.25 = (bf16[512,192]{0,1:T(8,128)(2,1)}, bf16[512,192]{0,1:T(8,128)(2,1)S(1)}, u32[]{:S(2)}) copy-start(bf16[512,192]{0,1:T(8,128)(2,1)S(1)} %get-tuple-element.50) | copy-start | bytes 589828
  61.9 7.3 %copy-start.22 = (bf16[1024,192]{0,1:T(8,128)(2,1)}, bf16[1024,192]{0,1:T(8,128)(2,1)S(1)}, u32[]{:S(2)}) copy-start(bf16[1024,192]{0,1:T(8,128)(2,1)S(1)} %get-tuple-element.54) | copy-start | bytes 1179652
  64.5 2.2 copy-start.32
  66.3 1.8 copy-start.16
  70.6 2.7 copy-start.15
  70.6 2.7 copy-start.36
  70.7 2.7 copy-start.27
  130.5 2.1 copy-start.19
  130.5 2.0 copy-start.42
  130.5 2.1 copy-start.37
  130.5 2.1 copy-start.40
  130.6 2.1 copy-start.46
  134.3 3.3 copy-start.11
  134.3 3.3 copy-start.29
  140.6 31.1 %copy-start.60 = (f32[1024,768]{1,0:T(8,128)}, f32[1024,768]{1,0:T(8,128)S(1)}, u32[]{:S(2)}) copy-start(f32[1024,768]{1,0:T(8,128)S(1)} %get-tuple-element.71) | copy-start | bytes 9437188
  142.1 29.6 %copy-start.59 = (bf16[1024,768]{1,0:T(8,128)(2,1)S(1)}, bf16[1024,768]{1,0:T(8,128)(2,1)}, u32[]{:S(2)}) copy-start(bf16[1024,768]{1,0:T(8,128)(2,1)} %all-gather.4.cloned.1.call-done) | copy-start | bytes 4718596
  179.3 142.9 %reduce-scatter.5.cloned.1.call-start = ((), (), s32[]{:S(2)}) async-start(), calls=%async_computation.3 | async-start | bytes 1966080 | tf_op jit(solution)/shard_map/reduce_scatter | solution.py:41
  182.1 30.6 %copy-start.9 = (bf16[8,96,768]{2,1,0:T(8,128)(2,1)S(1)}, bf16[8,96,768]{2,1,0:T(8,128)(2,1)}, u32[]{:S(2)}) copy-start(bf16[8,96,768]{2,1,0:T(8,128)(2,1)} %copy-done.8) | copy-start | bytes 3538948
  182.1 30.6 %copy-start.61 = (f32[1024,768]{1,0:T(8,128)S(1)}, f32[1024,768]{1,0:T(8,128)}, u32[]{:S(2)}) copy-start(f32[1024,768]{1,0:T(8,128)} %copy-done.60) | copy-start | bytes 9437188
  215.9 5.4 %copy-start.33 = (bf16[512,192]{0,1:T(8,128)(2,1)S(1)}, bf16[512,192]{0,1:T(8,128)(2,1)}, u32[]{:S(2)}) copy-start(bf16[512,192]{0,1:T(8,128)(2,1)} %get-tuple-element.53) | copy-start | bytes 589828
  215.9 5.4 %copy-start.17 = (f32[3,512,512]{1,2,0:T(8,128)S(1)}, f32[3,512,512]{1,2,0:T(8,128)}, u32[]{:S(2)}) copy-start(f32[3,512,512]{1,2,0:T(8,128)} %copy-done.16) | copy-start | bytes 9437188
  223.0 2.7 copy-start.28
  225.5 103.2 %all-gather.6.cloned.1.call-start = ((), (), s32[]{:S(2)}) async-start(), calls=%async_computation.4 | async-start | bytes 1474560 | tf_op jit(solution)/shard_map/all_gather | solution.py:656
  225.7 4.0 %slice-start = ((s8[6291456]{0:T(1024)(128)(4,1)}), s8[4194304]{0:T(1024)(128)(4,1)S(1)}, s32[]{:S(2)}) async-start(s8[6291456]{0:T(1024)(128)(4,1)} %bitcast.155), calls=%async_computation.6 | async-start | bytes 8388608
  225.7 4.7 %slice-start.1 = ((s8[6291456]{0:T(1024)(128)(4,1)}), s8[2097152]{0:T(1024)(128)(4,1)S(1)}, s32[]{:S(2)}) async-start(s8[6291456]{0:T(1024)(128)(4,1)} %bitcast.155), calls=%async_computation.7 | async-start | bytes 4194304
  233.0 1.9 copy-start.18
  238.1 3.5 %copy-start.14 = (bf16[8,96,576]{2,1,0:T(8,128)(2,1)S(1)}, bf16[8,96,576]{2,1,0:T(8,128)(2,1)}, u32[]{:S(2)}) copy-start(bf16[8,96,576]{2,1,0:T(8,128)(2,1)} %copy-done.12) | copy-start | bytes 2654212
  241.6 2.6 copy-start.4
  241.6 58.4 %copy-start.43 = (f32[256]{0:T(256)S(1)}, f32[256]{0:T(256)}, u32[]{:S(2)}) copy-start(f32[256]{0:T(256)} %broadcast_multiply_fusion.2) | copy-start | bytes 3076
  244.2 56.9 %copy-start.47 = (f32[1,8,96]{2,0,1:T(1,128)S(1)}, f32[1,8,96]{2,0,1:T(1,128)}, u32[]{:S(2)}) copy-start(f32[1,8,96]{2,0,1:T(1,128)} %stack.37) | copy-start | bytes 9220
  244.2 56.9 %copy-start.48 = (f32[1,8,96]{2,0,1:T(1,128)S(1)}, f32[1,8,96]{2,0,1:T(1,128)}, u32[]{:S(2)}) copy-start(f32[1,8,96]{2,0,1:T(1,128)} %stack.38) | copy-start | bytes 9220
  312.4 8.7 %copy-start.21 = (f32[256,768]{1,0:T(8,128)S(1)}, f32[256,768]{1,0:T(8,128)}, u32[]{:S(2)}) copy-start(f32[256,768]{1,0:T(8,128)} %copy-done.20) | copy-start | bytes 2359300
  312.4 8.7 %copy-start.24 = (bf16[1,256,768]{2,1,0:T(8,128)(2,1)S(1)}, bf16[1,256,768]{2,1,0:T(8,128)(2,1)}, u32[]{:S(2)}) copy-start(bf16[1,256,768]{2,1,0:T(8,128)(2,1)} %param.19) | copy-start | bytes 1179652
  312.4 8.7 %copy-start.50 = (f32[256]{0:T(256)S(1)}, f32[256]{0:T(256)}, u32[]{:S(2)}) copy-start(f32[256]{0:T(256)} %copy-done.49) | copy-start | bytes 3076
  332.2 7.8 %copy-start.1 = (bf16[384,768]{1,0:T(8,128)(2,1)S(1)}, bf16[384,768]{1,0:T(8,128)(2,1)}, u32[]{:S(2)}) copy-start(bf16[384,768]{1,0:T(8,128)(2,1)} %param.14) | copy-start | bytes 1769476
  (20 other events, 23.4 us)
Sparse Core Ops, SparseCore 0:
  57.5 39.0 all-gather.3
  179.4 42.0 reduce-scatter.6
  225.6 44.6 reduce-scatter.4
  300.6 28.1 all-gather.5
